TPU v7x, 32 devices: a whole 2x2x4 slice. The times are simulated.
32 devices in a mesh: tile: 8 (over y, x, core), win: 4 (over z).
Axes of the slice: x: 2, y: 2, z: 4, core: 2. Of those that a mesh axis runs over, the one named last changes fastest.
Arguments:
- signal: bfloat16 [4, 1024, 8192], P('win', 'tile'), may hold values from -6 to 6
- tile_list: int32 [16, 2], P('tile'), may hold values from -1 to 3, as said below
- band_mask: int32 [16, 256, 256], P('tile'), may hold values from 0 to 1, as said below
Outputs:
- stacked: float32 [16, 256, 1024], P('tile', 'win')
Inputs may be any that keep to these rules, and one draw needn't show every extreme that they name: `tile_list`: every band tile (row block i, column block j, i <= j <= i + 2, j < 4) stands in exactly one slot; the other slots hold -1 in both entries. Slots are placed at random. `band_mask`: zero on slots holding -1; on a tile it is 1 only where the two channels lie at most 448 apart and both are live.
All inputs are finite; a program needn't handle non-finite values.
Results may differ from a plain program's by a relative error of at most 0.0016.
Values may be sent and summed in bfloat16 or wider, within the bound.
A program may use at most 128 MiB of HBM per device.

v0:
```python
import math

import jax
import jax.numpy as jnp
from jax import lax
from jax.sharding import PartitionSpec as P

CB = 256
NT = 8192
F = 2048
F_LO = 64
LAGS = 4
LAG_STEP = 25


def lag_tables():
    lags = (jnp.arange(LAGS) - LAGS // 2) * LAG_STEP
    freqs = F_LO + jnp.arange(F)
    phase = jnp.mod(lags[:, None] * freqs[None, :], NT).astype(jnp.float32) * (2.0 * math.pi / NT)
    return (jnp.cos(phase), jnp.sin(phase))


def rotate_block(block, cosines, sines):
    values = block.astype(jnp.float32)
    real_part = values[:, :F]
    imag_part = values[:, F:]
    pieces = []
    for k in range(LAGS):
        new_real = real_part * cosines[k] + imag_part * sines[k]
        new_imag = imag_part * cosines[k] - real_part * sines[k]
        pieces.append(jnp.concatenate([new_real, new_imag], axis=-1).astype(jnp.bfloat16))
    return jnp.concatenate(pieces, axis=0)


def transform(rows):
    values = rows.astype(jnp.float32)
    values = values - jnp.mean(values, axis=-1, keepdims=True)
    times = jnp.arange(NT).astype(jnp.float32)
    window = 0.5 - 0.5 * jnp.cos(times * (2.0 * math.pi / NT))
    tapered = (values * window).astype(jnp.bfloat16)
    quarter = NT // 4
    freqs = F_LO + jnp.arange(F)
    times_here = jnp.arange(quarter)
    phase = jnp.mod(times_here[:, None] * freqs[None, :], NT).astype(jnp.float32) * (
        2.0 * math.pi / NT
    )
    table = jnp.concatenate([jnp.cos(phase), jnp.sin(phase)], axis=1).astype(jnp.bfloat16)
    real_total = jnp.zeros((rows.shape[0], F), jnp.float32)
    imag_total = jnp.zeros((rows.shape[0], F), jnp.float32)
    for quarter_index in range(4):
        part_rows = tapered[:, quarter_index * quarter : (quarter_index + 1) * quarter]
        product = jnp.dot(part_rows, table, preferred_element_type=jnp.float32)
        cos_part = product[:, :F]
        sin_part = product[:, F:]
        turns = jnp.mod(quarter_index * freqs, 4)[None, :]
        real_add = jnp.where(
            turns == 0,
            cos_part,
            jnp.where(turns == 1, -sin_part, jnp.where(turns == 2, -cos_part, sin_part)),
        )
        imag_add = jnp.where(
            turns == 0,
            -sin_part,
            jnp.where(turns == 1, -cos_part, jnp.where(turns == 2, sin_part, cos_part)),
        )
        real_total = real_total + real_add
        imag_total = imag_total + imag_add
    power = real_total * real_total + imag_total * imag_total
    level = jnp.mean(power, axis=-1, keepdims=True)
    scale = 1.0 / jnp.sqrt(power + 0.01 * level + 1e-06)
    return jnp.concatenate([real_total * scale, imag_total * scale], axis=-1).astype(jnp.bfloat16)


def shards(signal, tile_list, band_mask):
    white = transform(signal[0])
    slot_count = tile_list.shape[0]
    starts = jnp.maximum(tile_list, 0) * CB
    whole = lax.all_gather(white, "tile", axis=0, tiled=True)
    blocks = []
    for slot in range(slot_count):
        left = lax.dynamic_slice_in_dim(whole, starts[slot, 0], CB, 0)
        right = lax.dynamic_slice_in_dim(whole, starts[slot, 1], CB, 0)
        blocks.append((left, right))
    cosines, sines = lag_tables()
    rows_here = CB // lax.axis_size("win")
    norm = 1.0 / math.sqrt(F * lax.axis_size("win"))
    first_row = lax.axis_index("win") * rows_here
    mask_rows = lax.dynamic_slice_in_dim(band_mask, first_row, rows_here, 1)
    weights = jnp.tile(mask_rows.astype(jnp.float32), (1, 1, LAGS)) * norm
    terms = []
    for slot in range(slot_count):
        left, right = blocks[slot]
        rotated = rotate_block(right, cosines, sines)
        terms.append(
            lax.dot_general(
                left, rotated, (((1,), (1,)), ((), ())), preferred_element_type=jnp.float32
            )
        )
    summed = lax.psum_scatter(jnp.stack(terms, axis=0), "win", scatter_dimension=1, tiled=True)
    return summed * weights


def solution(mesh):
    placed = (P("win", "tile", None), P("tile", None), P("tile", None, None))
    return jax.shard_map(
        shards, mesh=mesh, in_specs=placed, out_specs=P("tile", "win", None), check_vma=False
    )
```

profile of v0, /device:TPU:0, one launch (start us, length us, event | category | flops | bytes accessed | tf_op | source)
XLA Modules:
  0.0 270.6 jit_solution(13925368951615675639)
XLA Ops:
  6.5 0.0 all-gather.2.cloned.1.call-start
  6.6 0.1 multiply_subtract_fusion
  6.7 1.9 convert_reduce_fusion
  8.7 0.0 copy-start
  8.7 67.1 %cosine_convert_fusion = (bf16[2048,2048]{1,0:T(8,128)(2,1)S(1)}, bf16[2048,2048]{1,0:T(8,128)(2,1)S(1)}) fusion(s32[2048]{0:T(1024)S(1)} %iota_add_fusion), kind=kLoop, calls=%fused_computation.8 | loop fusion | flops 67108864 | bytes 16785408 | tf_op jit(solution)/shard_map/convert.18
  75.8 0.0 copy-done
  75.8 0.6 fusion.40
  76.4 2.4 fusion.59
  78.9 3.7 %fusion.61 = f32[128,4096]{1,0:T(8,128)} fusion(bf16[128,8192]{1,0:T(8,128)(2,1)S(1)} %fusion.40, bf16[2048,2048]{1,0:T(8,128)(2,1)S(1)} %get-tuple-element.49, bf16[2048,2048]{1,0:T(8,128)(2,1)S(1)} %get-tuple-element.48), kind=kOutput, calls=%fused_computation.87 | convolution fusion | flops 2181038080 | bytes 19398656 | tf_op jit(solution)/shard_map/dot_general | solution.py:52
  82.6 0.6 broadcast_compare_fusion.6
  83.2 3.7 %fusion.63 = f32[128,4096]{1,0:T(8,128)} fusion(bf16[128,8192]{1,0:T(8,128)(2,1)S(1)} %fusion.40, bf16[2048,2048]{1,0:T(8,128)(2,1)S(1)} %get-tuple-element.49, bf16[2048,2048]{1,0:T(8,128)(2,1)S(1)} %get-tuple-element.48), kind=kOutput, calls=%fused_computation.89 | convolution fusion | flops 2181038080 | bytes 19398656 | tf_op jit(solution)/shard_map/dot_general | solution.py:52
  86.9 3.7 %fusion.65 = f32[128,4096]{1,0:T(8,128)} fusion(bf16[128,8192]{1,0:T(8,128)(2,1)S(1)} %fusion.40, bf16[2048,2048]{1,0:T(8,128)(2,1)S(1)} %get-tuple-element.49, bf16[2048,2048]{1,0:T(8,128)(2,1)S(1)} %get-tuple-element.48), kind=kOutput, calls=%fused_computation.91 | convolution fusion | flops 2181038080 | bytes 19398656 | tf_op jit(solution)/shard_map/dot_general | solution.py:52
  90.7 4.2 %fusion.58 = (f32[128]{0:T(128)S(1)}, f32[128,2048]{1,0:T(8,128)S(1)}, f32[128,2048]{1,0:T(8,128)S(1)}) fusion(pred[2048]{0:T(1024)(128)(4,1)S(1)} %get-tuple-element.54, f32[128,4096]{1,0:T(8,128)S(1)} %fusion.59, pred[2048]{0:T(1024)(128)(4,1)S(1)} %get-tuple-element.57, pred[2048]{0:T(1024)(128)(4,1)S(1)} %broadcast_compare_fusion.8, ...), kind=kLoop, calls=%fused_computation.84 | loop fusion | flops 9174912 | bytes 10504704 | tf_op jit(solution)/shard_map/reduce_sum | solution.py:69
  94.8 0.0 copy-start.1
  94.8 0.4 multiply_convert_fusion.1
  95.2 1.2 pad_maximum_fusion.2
  96.4 0.0 all-gather.2.cloned.1.call-update
  96.4 0.4 reduce-scatter.2.cloned.1.call-start
  96.9 0.0 copy-done.1
  96.9 0.7 fusion.86
  105.4 0.3 fusion.71
  105.8 47.9 %all-gather.2.cloned.1.call-done = bf16[1024,4096]{1,0:T(8,128)(2,1)} async-done(((bf16[128,4096]{1,0:T(8,128)(2,1)}), bf16[1024,4096]{1,0:T(8,128)(2,1)}) %all-gather.2.cloned.1.call-update) | async-done | bytes 8388624 | tf_op jit(solution)/shard_map/all_gather | solution.py:78
  153.7 3.5 %dynamic-slice_convert_fusion.1 = (f32[256,4096]{1,0:T(8,128)S(1)}, f32[256,4096]{1,0:T(8,128)S(1)}) fusion(bf16[1024,4096]{1,0:T(8,128)(2,1)} %all-gather.2.cloned.1.call-done, s32[]{:T(128)S(6)} %select_n.258, s32[]{:T(128)S(6)} %select_n.261), kind=kLoop, calls=%fused_computation.68 | loop fusion | flops 2097152 | bytes 12582920 | tf_op jit(solution)/shard_map/convert_element_type | solution.py:24
  157.2 3.6 %add_convert_fusion.3 = (bf16[256,2048]{1,0:T(8,128)(2,1)}, bf16[256,2048]{1,0:T(8,128)(2,1)}, bf16[256,2048]{1,0:T(8,128)(2,1)}, bf16[256,2048]{1,0:T(8,128)(2,...) fusion(f32[256,4096]{1,0:T(8,128)S(1)} %get-tuple-element.9, f32[2048]{0:T(1024)S(1)} %bitcast.34, ...), kind=kLoop, calls=%fused_computation.57 | loop fusion | flops 12582912 | bytes 10534912 | tf_op jit(solution)/shard_map/convert.6
  160.8 2.9 %add_convert_fusion.7 = (bf16[256,2048]{1,0:T(8,128)(2,1)S(1)}, bf16[256,2048]{1,0:T(8,128)(2,1)S(1)}, bf16[256,2048]{1,0:T(8,128)(2,1)S(1)}, bf16[256,2048]{1,0...) fusion(f32[256,4096]{1,0:T(8,128)S(1)} %get-tuple-element.8, f32[2048]{0:T(1024)S(1)} %bitcast.35, ...), kind=kLoop, calls=%fused_computation.67 | loop fusion | flops 12582912 | bytes 10534912 | tf_op jit(solution)/shard_map/convert.14
  163.6 3.4 %add_convert_fusion.4 = (bf16[256,2048]{1,0:T(8,128)(2,1)}, bf16[256,2048]{1,0:T(8,128)(2,1)}, bf16[256,2048]{1,0:T(8,128)(2,1)}, bf16[256,2048]{1,0:T(8,128)(2,1)}) fusion(f32[256,4096]{1,0:T(8,128)S(1)} %get-tuple-element.8, f32[2048]{0:T(1024)S(1)} %bitcast.37, f32[2048]{0:T(1024)S(1)} %bitcast.36, f32[256,4096]{1,0:T(8,128)S(1)} %get-tuple-element.9), kind=kLoop, calls=%fused_computation.61 | loop fusion | flops 8388608 | bytes 12599296 | tf_op jit(solution)/shard_map/convert.8
  167.0 15.7 %fusion.43 = f32[1,256,1024]{2,1,0:T(8,128)} fusion(bf16[256,2048]{1,0:T(8,128)(2,1)} %get-tuple-element.44, bf16[256,2048]{1,0:T(8,128)(2,1)} %get-tuple-element.45, bf16[256,2048]{1,0:T(8,128)(2,1)} %get-tuple-element.32, bf16[256,2048]{1,0:T(8,128)(2,1)} %get-tuple-element.33, bf16[256,2048]{1,0:T(8,128)(2,1)} %get-tuple-element.30, ...), kind=kOutput, calls=%fused_computation.70 | convolution fusion | flops 2214592512 | bytes 11534340 | tf_op jit(solution)/shard_map/dot_general | solution.py:95
  182.7 31.8 %fusion.48 = f32[1,256,1024]{2,1,0:T(8,128)} fusion(bf16[256,2048]{1,0:T(8,128)(2,1)} %get-tuple-element.17, bf16[256,2048]{1,0:T(8,128)(2,1)} %get-tuple-element.16, bf16[256,2048]{1,0:T(8,128)(2,1)} %get-tuple-element.28, bf16[256,2048]{1,0:T(8,128)(2,1)} %get-tuple-element.29, bf16[256,2048]{1,0:T(8,128)(2,1)S(1)} %get-tuple-element.26, ...), kind=kOutput, calls=%fused_computation.71 | convolution fusion | flops 2214592512 | bytes 11534340 | tf_op jit(solution)/shard_map/dot_general | solution.py:95
  214.6 3.1 %pad_maximum_fusion.1 = f32[2,256,1024]{2,1,0:T(8,128)} fusion(f32[1,256,1024]{2,1,0:T(8,128)} %fusion.43, f32[1,256,1024]{2,1,0:T(8,128)} %fusion.48), kind=kLoop, calls=%fused_computation.49 | loop fusion | flops 524288 | bytes 4194304 | tf_op jit(solution)/shard_map/stack | solution.py:99
  217.7 0.0 reduce-scatter.2.cloned.1.call-update
  217.7 0.9 convert_multiply_fusion
  218.6 0.1 tile.2
  218.7 0.3 mul.875
  219.0 42.7 %reduce-scatter.2.cloned.1.call-done = f32[2,64,1024]{2,1,0:T(8,128)} async-done(((f32[2,256,1024]{2,1,0:T(8,128)}), f32[2,64,1024]{2,1,0:T(8,128)}) %reduce-scatter.2.cloned.1.call-update) | async-done | bytes 524304 | tf_op jit(solution)/shard_map/reduce_scatter | solution.py:99
  261.7 1.9 mul.876
  (10 shorter events, 0.1 us)
Async XLA Ops:
  6.5 147.1 %all-gather.2.cloned.1.call-start = ((), (), s32[]{:S(2)}) async-start(), calls=%async_computation.1 | async-start | bytes 9437184 | tf_op jit(solution)/shard_map/all_gather | solution.py:78
  8.7 67.1 %copy-start = (bf16[1,128,8192]{2,1,0:T(8,128)(2,1)S(1)}, bf16[1,128,8192]{2,1,0:T(8,128)(2,1)}, u32[]{:S(2)}) copy-start(bf16[1,128,8192]{2,1,0:T(8,128)(2,1)} %param.3) | copy-start | bytes 6291460
  94.8 2.1 copy-start.1
  96.4 165.3 %reduce-scatter.2.cloned.1.call-start = ((), (), s32[]{:S(2)}) async-start(), calls=%async_computation.2 | async-start | bytes 2621440 | tf_op jit(solution)/shard_map/reduce_scatter | solution.py:99
Sparse Core Ops, SparseCore 0:
  96.5 57.0 all-gather.1
  217.8 43.8 reduce-scatter.1
where the time goes:
time: 275 us; the launch traced here: 271 us
  other arithmetic  95.8 us (35%)
  waiting for transfers between devices  90.6 us (33%)
  matrix products  61.2 us (22%)
  between operations  21.5 us (8%)
    another operation x5, other arithmetic  77.3 us
    all_gather x1, waiting for transfers between devices, shards(): whole = lax.all_gather(white, 'tile', axis=0, tiled=True)  47.9 us
    dot_general x2, matrix products, shards(): lax.dot_general(left, rotated, (((1,), (1,)), ((), ())), preferred_elemen...  47.6 us
    reduce_scatter x1, waiting for transfers between devices, shards(): lax.psum_scatter(jnp.stack(terms, axis=0), 'win', scatter_dimension=1, ti...  42.7 us
    dot_general x4, matrix products, transform(): product = jnp.dot(part_rows, table, preferred_element_type=jnp.float32)  13.6 us
  transfers between devices with their start and end apart: 2, of which 2 were waited for; matrix products, arithmetic and copies ran while one was open for 1% of the time, Pallas kernels for 0%

commit v1 on v0

--- a/solution.py
+++ b/solution.py
@@ -2,6 +2,8 @@
 
 import jax
 import jax.numpy as jnp
+import ml_dtypes
+import numpy as np
 from jax import lax
 from jax.sharding import PartitionSpec as P
 
@@ -32,6 +34,12 @@
     return jnp.concatenate(pieces, axis=0)
 
 
+def quarter_table():
+    phase = (np.arange(NT // 4)[:, None] * (F_LO + np.arange(F))[None, :]) % NT
+    angle = phase * (2.0 * math.pi / NT)
+    return np.concatenate([np.cos(angle), np.sin(angle)], axis=1).astype(ml_dtypes.bfloat16)
+
+
 def transform(rows):
     values = rows.astype(jnp.float32)
     values = values - jnp.mean(values, axis=-1, keepdims=True)
@@ -40,11 +48,7 @@
     tapered = (values * window).astype(jnp.bfloat16)
     quarter = NT // 4
     freqs = F_LO + jnp.arange(F)
-    times_here = jnp.arange(quarter)
-    phase = jnp.mod(times_here[:, None] * freqs[None, :], NT).astype(jnp.float32) * (
-        2.0 * math.pi / NT
-    )
-    table = jnp.concatenate([jnp.cos(phase), jnp.sin(phase)], axis=1).astype(jnp.bfloat16)
+    table = jnp.asarray(quarter_table())
     real_total = jnp.zeros((rows.shape[0], F), jnp.float32)
     imag_total = jnp.zeros((rows.shape[0], F), jnp.float32)
     for quarter_index in range(4):

time: 275 us -> 219 us (0.80)
  other arithmetic: 95.8 us -> 25.6 us
  matrix products: 61.2 us -> 74.2 us
    another operation x5 -> x4, other arithmetic: 77.3 us -> 10.5 us
    dot_general x2, matrix products: 47.6 us -> 58.7 us  [shards(): lax.dot_general(left, rotated, (((1,), (1,)), ((), ())), preferred_elemen...]
    reduce_sum x1, other arithmetic: 4.16 us -> 1.33 us  [transform(): level = jnp.mean(power, axis=-1, keepdims=True)]
where the time goes in v1:
time: 219 us; the launch traced here: 216 us
  waiting for transfers between devices  91 us (42%)
  matrix products  74.2 us (34%)
  other arithmetic  25.6 us (12%)
  between operations  21.6 us (10%)
  local copies, waits for them, and re-layouts  3.33 us (2%)
    dot_general x2, matrix products, shards(): lax.dot_general(left, rotated, (((1,), (1,)), ((), ())), preferred_elemen...  58.7 us
    all_gather x1, waiting for transfers between devices, shards(): whole = lax.all_gather(white, 'tile', axis=0, tiled=True)  48.3 us
    reduce_scatter x1, waiting for transfers between devices, shards(): lax.psum_scatter(jnp.stack(terms, axis=0), 'win', scatter_dimension=1, ti...  42.7 us
    dot_general x4, matrix products, transform(): product = jnp.dot(part_rows, table, preferred_element_type=jnp.float32)  15.5 us
    another operation x4, other arithmetic  10.5 us
  transfers between devices with their start and end apart: 2, of which 2 were waited for; matrix products, arithmetic and copies ran while one was open for 1% of the time, Pallas kernels for 0%

profile of v1, /device:TPU:0, one launch (start us, length us, event | category | flops | bytes accessed | tf_op | source)
XLA Modules:
  0.0 215.8 jit_solution(13355530174358170597)
XLA Ops:
  6.5 0.0 copy-start.1
  6.5 0.0 all-gather.2.cloned.1.call-start
  6.6 0.1 multiply_subtract_fusion
  6.7 2.1 convert_reduce_fusion
  8.8 0.0 copy-done.1
  8.8 0.6 fusion.34
  9.4 0.0 copy-start
  9.4 8.3 %fusion.53 = f32[128,4096]{1,0:T(8,128)S(1)} fusion(bf16[2048,4096]{1,0:T(8,128)(2,1)} %constant.104.clone, bf16[128,8192]{1,0:T(8,128)(2,1)S(1)} %fusion.34), kind=kOutput, calls=%fused_computation.73 | convolution fusion | flops 2147483648 | bytes 19398656 | tf_op jit(solution)/shard_map/dot_general | solution.py:56
  17.7 2.2 %copy-done = bf16[2048,4096]{1,0:T(8,128)(2,1)S(1)} copy-done((bf16[2048,4096]{1,0:T(8,128)(2,1)S(1)}, bf16[2048,4096]{1,0:T(8,128)(2,1)}, u32[]{:S(2)}) %copy-start) | copy-done | bytes 16777240
  19.9 2.4 %fusion.55 = f32[128,4096]{1,0:T(8,128)S(1)} fusion(bf16[2048,4096]{1,0:T(8,128)(2,1)S(1)} %copy-done, bf16[128,8192]{1,0:T(8,128)(2,1)S(1)} %fusion.34), kind=kOutput, calls=%fused_computation.75 | convolution fusion | flops 2147483648 | bytes 19398656 | tf_op jit(solution)/shard_map/dot_general | solution.py:56
  22.4 2.4 %fusion.57 = f32[128,4096]{1,0:T(8,128)S(1)} fusion(bf16[2048,4096]{1,0:T(8,128)(2,1)S(1)} %copy-done, bf16[128,8192]{1,0:T(8,128)(2,1)S(1)} %fusion.34), kind=kOutput, calls=%fused_computation.77 | convolution fusion | flops 2147483648 | bytes 19398656 | tf_op jit(solution)/shard_map/dot_general | solution.py:56
  24.8 2.4 %fusion.59 = f32[128,4096]{1,0:T(8,128)S(1)} fusion(bf16[2048,4096]{1,0:T(8,128)(2,1)S(1)} %copy-done, bf16[128,8192]{1,0:T(8,128)(2,1)S(1)} %fusion.34), kind=kOutput, calls=%fused_computation.79 | convolution fusion | flops 2147483648 | bytes 19398656 | tf_op jit(solution)/shard_map/dot_general | solution.py:56
  27.2 1.3 fusion.52
  28.5 0.7 multiply_convert_fusion.1
  29.2 0.0 copy-start.2
  29.2 1.2 pad_maximum_fusion.1
  30.4 0.0 all-gather.2.cloned.1.call-update
  30.4 0.0 reduce-scatter.2.cloned.1.call-start
  30.5 0.0 copy-done.2
  30.5 0.7 fusion.80
  39.0 0.3 fusion.65
  39.4 48.3 %all-gather.2.cloned.1.call-done = bf16[1024,4096]{1,0:T(8,128)(2,1)} async-done(((bf16[128,4096]{1,0:T(8,128)(2,1)}), bf16[1024,4096]{1,0:T(8,128)(2,1)}) %all-gather.2.cloned.1.call-update) | async-done | bytes 8388624 | tf_op jit(solution)/shard_map/all_gather | solution.py:82
  87.7 3.5 %dynamic-slice_convert_fusion.1 = (f32[256,4096]{1,0:T(8,128)S(1)}, f32[256,4096]{1,0:T(8,128)S(1)}) fusion(bf16[1024,4096]{1,0:T(8,128)(2,1)} %all-gather.2.cloned.1.call-done, s32[]{:T(128)S(6)} %select_n.249, s32[]{:T(128)S(6)} %select_n.252), kind=kLoop, calls=%fused_computation.56 | loop fusion | flops 2097152 | bytes 12582920 | tf_op jit(solution)/shard_map/convert_element_type | solution.py:26
  91.2 3.6 %add_convert_fusion.3 = (bf16[256,2048]{1,0:T(8,128)(2,1)}, bf16[256,2048]{1,0:T(8,128)(2,1)}, bf16[256,2048]{1,0:T(8,128)(2,1)}, bf16[256,2048]{1,0:T(8,128)(2,...) fusion(f32[256,4096]{1,0:T(8,128)S(1)} %get-tuple-element.9, f32[2048]{0:T(1024)S(1)} %bitcast.38, ...), kind=kLoop, calls=%fused_computation.45 | loop fusion | flops 12582912 | bytes 10534912 | tf_op jit(solution)/shard_map/convert.6
  94.7 2.9 %add_convert_fusion.7 = (bf16[256,2048]{1,0:T(8,128)(2,1)S(1)}, bf16[256,2048]{1,0:T(8,128)(2,1)S(1)}, bf16[256,2048]{1,0:T(8,128)(2,1)S(1)}, bf16[256,2048]{1,0...) fusion(f32[256,4096]{1,0:T(8,128)S(1)} %get-tuple-element.8, f32[2048]{0:T(1024)S(1)} %bitcast.39, ...), kind=kLoop, calls=%fused_computation.55 | loop fusion | flops 12582912 | bytes 10534912 | tf_op jit(solution)/shard_map/convert.14
  97.6 3.4 %add_convert_fusion.4 = (bf16[256,2048]{1,0:T(8,128)(2,1)}, bf16[256,2048]{1,0:T(8,128)(2,1)}, bf16[256,2048]{1,0:T(8,128)(2,1)}, bf16[256,2048]{1,0:T(8,128)(2,1)}) fusion(f32[256,4096]{1,0:T(8,128)S(1)} %get-tuple-element.8, f32[2048]{0:T(1024)S(1)} %bitcast.41, f32[2048]{0:T(1024)S(1)} %bitcast.40, f32[256,4096]{1,0:T(8,128)S(1)} %get-tuple-element.9), kind=kLoop, calls=%fused_computation.49 | loop fusion | flops 8388608 | bytes 12599296 | tf_op jit(solution)/shard_map/convert.8
  101.0 15.7 %fusion.37 = f32[1,256,1024]{2,1,0:T(8,128)} fusion(bf16[256,2048]{1,0:T(8,128)(2,1)} %get-tuple-element.44, bf16[256,2048]{1,0:T(8,128)(2,1)} %get-tuple-element.45, bf16[256,2048]{1,0:T(8,128)(2,1)} %get-tuple-element.32, bf16[256,2048]{1,0:T(8,128)(2,1)} %get-tuple-element.33, bf16[256,2048]{1,0:T(8,128)(2,1)} %get-tuple-element.30, ...), kind=kOutput, calls=%fused_computation.58 | convolution fusion | flops 2214592512 | bytes 11534340 | tf_op jit(solution)/shard_map/dot_general | solution.py:99
  116.7 43.0 %fusion.42 = f32[1,256,1024]{2,1,0:T(8,128)} fusion(bf16[256,2048]{1,0:T(8,128)(2,1)} %get-tuple-element.17, bf16[256,2048]{1,0:T(8,128)(2,1)} %get-tuple-element.16, bf16[256,2048]{1,0:T(8,128)(2,1)} %get-tuple-element.28, bf16[256,2048]{1,0:T(8,128)(2,1)} %get-tuple-element.29, bf16[256,2048]{1,0:T(8,128)(2,1)S(1)} %get-tuple-element.26, ...), kind=kOutput, calls=%fused_computation.59 | convolution fusion | flops 2214592512 | bytes 11534340 | tf_op jit(solution)/shard_map/dot_general | solution.py:99
  159.7 3.1 %pad_maximum_fusion = f32[2,256,1024]{2,1,0:T(8,128)} fusion(f32[1,256,1024]{2,1,0:T(8,128)} %fusion.37, f32[1,256,1024]{2,1,0:T(8,128)} %fusion.42), kind=kLoop, calls=%fused_computation.37 | loop fusion | flops 524288 | bytes 4194304 | tf_op jit(solution)/shard_map/stack | solution.py:103
  162.8 0.0 reduce-scatter.2.cloned.1.call-update
  162.8 0.9 convert_multiply_fusion
  163.8 0.1 tile.2
  163.9 0.3 mul.843
  164.1 42.7 %reduce-scatter.2.cloned.1.call-done = f32[2,64,1024]{2,1,0:T(8,128)} async-done(((f32[2,256,1024]{2,1,0:T(8,128)}), f32[2,64,1024]{2,1,0:T(8,128)}) %reduce-scatter.2.cloned.1.call-update) | async-done | bytes 524304 | tf_op jit(solution)/shard_map/reduce_scatter | solution.py:103
  206.8 1.9 mul.844
  (11 shorter events, 0.2 us)
Async XLA Ops:
  6.5 2.3 %copy-start.1 = (bf16[1,128,8192]{2,1,0:T(8,128)(2,1)S(1)}, bf16[1,128,8192]{2,1,0:T(8,128)(2,1)}, u32[]{:S(2)}) copy-start(bf16[1,128,8192]{2,1,0:T(8,128)(2,1)} %param.4) | copy-start | bytes 6291460
  6.5 81.1 %all-gather.2.cloned.1.call-start = ((), (), s32[]{:S(2)}) async-start(), calls=%async_computation.1 | async-start | bytes 9437184 | tf_op jit(solution)/shard_map/all_gather | solution.py:82
  9.4 10.5 %copy-start = (bf16[2048,4096]{1,0:T(8,128)(2,1)S(1)}, bf16[2048,4096]{1,0:T(8,128)(2,1)}, u32[]{:S(2)}) copy-start(bf16[2048,4096]{1,0:T(8,128)(2,1)} %constant.104.clone) | copy-start | bytes 50331652
  29.2 1.3 copy-start.2
  30.4 176.4 %reduce-scatter.2.cloned.1.call-start = ((), (), s32[]{:S(2)}) async-start(), calls=%async_computation.2 | async-start | bytes 2621440 | tf_op jit(solution)/shard_map/reduce_scatter | solution.py:103
Sparse Core Ops, SparseCore 0:
  30.5 57.0 all-gather.1
  163.0 43.8 reduce-scatter.1

commit v2 on v1

v2 whole, which is shorter than its diff:
```python
import functools
import math

import jax
import jax.numpy as jnp
import ml_dtypes
import numpy as np
from jax import lax
from jax.experimental import pallas as pl
from jax.experimental.pallas import tpu as pltpu
from jax.sharding import PartitionSpec as P

CB = 256
NT = 8192
F = 2048
F_LO = 64
LAGS = 4
LAG_STEP = 25


def quarter_table():
    phase = (np.arange(NT // 4)[:, None] * (F_LO + np.arange(F))[None, :]) % NT
    angle = phase * (2.0 * math.pi / NT)
    return np.concatenate([np.cos(angle), np.sin(angle)], axis=1).astype(ml_dtypes.bfloat16)


def transform(rows):
    values = rows.astype(jnp.float32)
    values = values - jnp.mean(values, axis=-1, keepdims=True)
    times = jnp.arange(NT).astype(jnp.float32)
    window = 0.5 - 0.5 * jnp.cos(times * (2.0 * math.pi / NT))
    tapered = (values * window).astype(jnp.bfloat16)
    quarter = NT // 4
    freqs = F_LO + jnp.arange(F)
    table = jnp.asarray(quarter_table())
    real_total = jnp.zeros((rows.shape[0], F), jnp.float32)
    imag_total = jnp.zeros((rows.shape[0], F), jnp.float32)
    for quarter_index in range(4):
        part_rows = tapered[:, quarter_index * quarter : (quarter_index + 1) * quarter]
        product = jnp.dot(part_rows, table, preferred_element_type=jnp.float32)
        cos_part = product[:, :F]
        sin_part = product[:, F:]
        turns = jnp.mod(quarter_index * freqs, 4)[None, :]
        real_add = jnp.where(
            turns == 0,
            cos_part,
            jnp.where(turns == 1, -sin_part, jnp.where(turns == 2, -cos_part, sin_part)),
        )
        imag_add = jnp.where(
            turns == 0,
            -sin_part,
            jnp.where(turns == 1, -cos_part, jnp.where(turns == 2, sin_part, cos_part)),
        )
        real_total = real_total + real_add
        imag_total = imag_total + imag_add
    power = real_total * real_total + imag_total * imag_total
    level = jnp.mean(power, axis=-1, keepdims=True)
    scale = 1.0 / jnp.sqrt(power + 0.01 * level + 1e-06)
    return jnp.concatenate([real_total * scale, imag_total * scale], axis=-1).astype(jnp.bfloat16)


def lag_tables():
    lags = (np.arange(LAGS) - LAGS // 2) * LAG_STEP
    phase = ((lags[:, None] * (F_LO + np.arange(F))[None, :]) % NT) * (2.0 * math.pi / NT)
    return np.cos(phase).astype(np.float32), np.sin(phase).astype(np.float32)


def correlate_kernel(
    blocks, windows,
    white, pairs, weights, cosines, sines,
    out,
    left, left_next, right_far, rotated, product, outgoing, incoming, own_rows, gathered,
    half_send, half_recv, local_sem, win_send, win_recv, tile_send, tile_recv, pass_send, pass_recv,
):
    half = white.shape[0]
    rows_here = CB // windows
    tile = lax.axis_index("tile")
    win = lax.axis_index("win")
    chip, core = tile // 2, tile % 2
    sibling = chip * 2 + (1 - core)
    my_half = pl.ds(pl.multiple_of(core * half, half), half)

    def holds(which):
        even = which % 2 == 0
        far = which + 2 < blocks
        return [which >= 0, even, far, jnp.logical_and(even, far)]

    mine = holds(chip)
    even, far = mine[1], mine[2]

    def remote(src, dst, send, recv, **where):
        return pltpu.make_async_remote_copy(
            src_ref=src, dst_ref=dst, send_sem=send, recv_sem=recv,
            device_id=where, device_id_type=pl.DeviceIdType.MESH,
        )

    def chip_ahead(step):
        return lax.rem(chip + step, blocks)

    barrier = pltpu.get_barrier_semaphore()
    pl.semaphore_signal(barrier, inc=1, device_id={"tile": sibling}, device_id_type=pl.DeviceIdType.MESH)
    for step in range(1, blocks):
        pl.semaphore_signal(
            barrier, inc=1, device_id={"tile": chip_ahead(step) * 2 + core}, device_id_type=pl.DeviceIdType.MESH
        )
    for step in range(1, windows):
        pl.semaphore_signal(
            barrier, inc=1, device_id={"win": lax.rem(win + step, windows)}, device_id_type=pl.DeviceIdType.MESH
        )
    pl.semaphore_wait(barrier, blocks + windows - 1)

    odd_chip = chip % 2 == 1
    late_chip = chip >= 2
    before = lax.rem(chip + blocks - 1, blocks) * 2 + core
    before2 = lax.rem(chip + blocks - 2, blocks) * 2 + core
    to_before = remote(white, left_next.at[my_half], half_send.at[0], half_recv.at[0], tile=before)
    to_before2 = remote(white, right_far, half_send.at[1], half_recv.at[1], tile=before2)
    to_sibling = remote(white, left.at[my_half], half_send.at[2], half_recv.at[2], tile=sibling)
    pass_on = remote(
        left_next.at[my_half], left_next.at[my_half], half_send.at[3], half_recv.at[3], tile=sibling
    )
    keep = pltpu.make_async_copy(white, left.at[my_half], local_sem)

    pl.when(odd_chip)(to_before.start)
    pl.when(late_chip)(to_before2.start)
    to_sibling.start()
    keep.start()

    def rotate(read):
        width = 512
        for part in range(F // width):
            real_cols = pl.ds(part * width, width)
            imag_cols = pl.ds(F + part * width, width)
            real_part = read(real_cols).astype(jnp.float32)
            imag_part = read(imag_cols).astype(jnp.float32)
            for k in range(LAGS):
                c = cosines[pl.ds(k, 1), real_cols]
                s = sines[pl.ds(k, 1), real_cols]
                lag_rows = pl.ds(k * half, half)
                rotated[lag_rows, real_cols] = (real_part * c + imag_part * s).astype(jnp.bfloat16)
                rotated[lag_rows, imag_cols] = (imag_part * c - real_part * s).astype(jnp.bfloat16)

    def win_copy(t, step):
        peer = lax.rem(win + step, windows)
        rows = pl.ds(pl.multiple_of(peer * rows_here, rows_here), rows_here)
        return remote(
            outgoing.at[t, rows], incoming.at[t, step - 1],
            win_send.at[t, step - 1], win_recv.at[t, step - 1], win=peer,
        )

    def spread(index):
        return 1.0 + index.astype(jnp.float32) / windows

    def multiply(t, rows_ref):
        for part in range(LAGS * half // 256):
            cols = pl.ds(part * 256, 256)
            product[:, cols] = lax.dot_general(
                rows_ref[...], rotated[cols, :], (((1,), (1,)), ((), ())),
                preferred_element_type=jnp.float32,
            )
        outgoing[t] = (product[...] * spread(win)).astype(jnp.bfloat16)
        own_rows[t] = product[pl.ds(pl.multiple_of(win * rows_here, rows_here), rows_here), :]
        for step in range(1, windows):
            win_copy(t, step).start()

    def tile_copy(t, step):
        spot = gathered.at[core, chip, t]
        return remote(
            spot, spot, tile_send.at[t, step - 1], tile_recv.at[t, step - 1], tile=chip_ahead(step) * 2 + core
        )

    def pass_copy(t, step):
        spot = gathered.at[core, chip_ahead(blocks - step), t]
        return remote(spot, spot, pass_send.at[t, step], pass_recv.at[t, step], tile=sibling)

    def collect(t):
        total = own_rows[t]
        for step in range(1, windows):
            win_copy(t, step).wait_recv()
            sender = lax.rem(win + windows - step, windows)
            total = total + incoming[t, step - 1].astype(jnp.float32) / spread(sender)
        gathered[core, chip, t] = total
        for step in range(1, blocks):
            tile_copy(t, step).start()
        pass_copy(t, 0).start()

    keep.wait()
    rotate(lambda cols: white[:, cols])
    to_sibling.wait_recv()
    multiply(0, left)

    @pl.when(even)
    def _():
        to_before.wait_recv()
        pass_on.start()
        rotate(lambda cols: left_next[my_half, cols])
        multiply(1, left)

    collect(0)

    @pl.when(far)
    def _():
        to_before2.wait_recv()
        rotate(lambda cols: right_far[:, cols])
        multiply(2, left)

    @pl.when(even)
    def _():
        pass_on.wait_recv()

    @pl.when(mine[3])
    def _():
        multiply(3, left_next)

    for t in range(1, 4):
        pl.when(mine[t])(functools.partial(collect, t))

    for t in range(4):
        for step in range(1, blocks):

            @pl.when(holds(chip_ahead(blocks - step))[t])
            def _():
                tile_copy(t, step).wait_recv()
                pass_copy(t, step).start()

    for t in range(4):
        for step in range(blocks):

            @pl.when(holds(chip_ahead(blocks - step))[t])
            def _():
                pass_copy(t, step).wait_recv()

    for slot in range(out.shape[0]):
        row_block = pairs[slot, 0]
        distance = pairs[slot, 1] - row_block
        live = row_block >= 0
        row_block = jnp.maximum(row_block, 0)
        step_in = jnp.logical_and(distance == 1, row_block % 2 == 1)
        place = jnp.where(step_in, row_block - 1, row_block)
        which = jnp.where(step_in, 3, distance)
        for side in range(2):
            values = gathered[side, place, which]
            side_cols = pl.ds(side * half, half)
            factor = weights[slot, :, side_cols]
            for k in range(LAGS):
                piece = values[:, k * half : (k + 1) * half] * factor
                out[slot, :, pl.ds(k * CB + side * half, half)] = jnp.where(live, piece, 0.0)

    pl.when(odd_chip)(to_before.wait_send)
    pl.when(late_chip)(to_before2.wait_send)
    to_sibling.wait_send()
    pl.when(even)(pass_on.wait_send)

    for t in range(4):

        @pl.when(mine[t])
        def _():
            for step in range(1, windows):
                win_copy(t, step).wait_send()
            for step in range(1, blocks):
                tile_copy(t, step).wait_send()

        for step in range(blocks):
            pl.when(holds(chip_ahead(blocks - step))[t])(pass_copy(t, step).wait_send)


def shards(signal, tile_list, band_mask):
    white = transform(signal[0])
    slot_count = tile_list.shape[0]
    windows = lax.axis_size("win")
    half = white.shape[0]
    blocks = lax.axis_size("tile") * half // CB
    rows_here = CB // windows
    norm = 1.0 / math.sqrt(F * windows)
    first_row = lax.axis_index("win") * rows_here
    mask_rows = lax.dynamic_slice_in_dim(band_mask, first_row, rows_here, 1)
    weights = mask_rows.astype(jnp.float32) * norm
    cosines, sines = lag_tables()
    vmem = pl.BlockSpec(memory_space=pltpu.VMEM)
    dma = pltpu.SemaphoreType.DMA
    width = LAGS * half
    return pl.pallas_call(
        functools.partial(correlate_kernel, blocks, windows),
        out_shape=jax.ShapeDtypeStruct((slot_count, rows_here, LAGS * CB), jnp.float32),
        in_specs=[vmem, pl.BlockSpec(memory_space=pltpu.SMEM), vmem, vmem, vmem],
        out_specs=vmem,
        scratch_shapes=[
            pltpu.VMEM((CB, 2 * F), jnp.bfloat16),
            pltpu.VMEM((CB, 2 * F), jnp.bfloat16),
            pltpu.VMEM((half, 2 * F), jnp.bfloat16),
            pltpu.VMEM((width, 2 * F), jnp.bfloat16),
            pltpu.VMEM((CB, width), jnp.float32),
            pltpu.VMEM((4, CB, width), jnp.bfloat16),
            pltpu.VMEM((4, windows - 1, rows_here, width), jnp.bfloat16),
            pltpu.VMEM((4, rows_here, width), jnp.float32),
            pltpu.VMEM((2, blocks, 4, rows_here, width), jnp.float32),
            dma((4,)), dma((4,)), dma,
            dma((4, windows - 1)), dma((4, windows - 1)),
            dma((4, blocks - 1)), dma((4, blocks - 1)),
            dma((4, blocks)), dma((4, blocks)),
        ],
        compiler_params=pltpu.CompilerParams(
            collective_id=0, has_side_effects=True, vmem_limit_bytes=48 * 1024 * 1024
        ),
        cost_estimate=pl.CostEstimate(flops=5 * 10**9, bytes_accessed=4 * 10**6, transcendentals=0),
    )(white, tile_list, weights, cosines, sines)


def solution(mesh):
    placed = (P("win", "tile", None), P("tile", None), P("tile", None, None))
    return jax.shard_map(
        shards, mesh=mesh, in_specs=placed, out_specs=P("tile", "win", None), check_vma=False
    )
```

time: 219 us -> 83.4 us (0.38)
  the two profiles are of different devices: /device:TPU:0 before, /device:TPU:15 now
where the time goes in v2:
time: 83.4 us; the launch traced here: 83.2 us
  Pallas kernels  58.6 us (70%)
  matrix products  15.5 us (19%)
  other arithmetic  5.9 us (7%)
  local copies, waits for them, and re-layouts  3.07 us (4%)
    pallas_call x1, Pallas kernels, shards(): pl.pallas_call(functools.partial(correlate_kernel, blocks, windows), out_...  58.6 us
    dot_general x4, matrix products, transform(): product = jnp.dot(part_rows, table, preferred_element_type=jnp.float32)  15.5 us
    unnamed x11, local copies, waits for them, and re-layouts  3.07 us
    reduce_sum x1, other arithmetic, transform(): values = values - jnp.mean(values, axis=-1, keepdims=True)  2.07 us

profile of v2, /device:TPU:15, one launch (start us, length us, event | category | flops | bytes accessed | tf_op | source)
XLA Modules:
  0.0 83.2 jit_solution(17152476415594360160)
XLA Ops:
  0.0 0.0 copy-start.4
  0.0 0.1 multiply_subtract_fusion
  0.1 2.1 %convert_reduce_fusion = f32[128]{0:T(128)S(1)} fusion(bf16[1,128,8192]{2,1,0:T(8,128)(2,1)} %param.6), kind=kLoop, calls=%fused_computation | loop fusion | flops 2097024 | bytes 2097664 | tf_op jit(solution)/shard_map/reduce_sum | solution.py:29
  2.2 0.0 copy-done.4
  2.2 0.6 fusion.2
  2.9 0.0 copy-start.3
  2.9 8.3 %fusion.11 = f32[128,4096]{1,0:T(8,128)S(1)} fusion(bf16[2048,4096]{1,0:T(8,128)(2,1)} %constant.84.clone, bf16[128,8192]{1,0:T(8,128)(2,1)S(1)} %fusion.2), kind=kOutput, calls=%fused_computation.20 | convolution fusion | flops 2147483648 | bytes 19398656 | tf_op jit(solution)/shard_map/dot_general | solution.py:40
  11.2 2.2 %copy-done.3 = bf16[2048,4096]{1,0:T(8,128)(2,1)S(1)} copy-done((bf16[2048,4096]{1,0:T(8,128)(2,1)S(1)}, bf16[2048,4096]{1,0:T(8,128)(2,1)}, u32[]{:S(2)}) %copy-start.3) | copy-done | bytes 16777240
  13.4 2.4 %fusion.13 = f32[128,4096]{1,0:T(8,128)S(1)} fusion(bf16[2048,4096]{1,0:T(8,128)(2,1)S(1)} %copy-done.3, bf16[128,8192]{1,0:T(8,128)(2,1)S(1)} %fusion.2), kind=kOutput, calls=%fused_computation.22 | convolution fusion | flops 2147483648 | bytes 19398656 | tf_op jit(solution)/shard_map/dot_general | solution.py:40
  15.8 2.4 %fusion.15 = f32[128,4096]{1,0:T(8,128)S(1)} fusion(bf16[2048,4096]{1,0:T(8,128)(2,1)S(1)} %copy-done.3, bf16[128,8192]{1,0:T(8,128)(2,1)S(1)} %fusion.2), kind=kOutput, calls=%fused_computation.24 | convolution fusion | flops 2147483648 | bytes 19398656 | tf_op jit(solution)/shard_map/dot_general | solution.py:40
  18.2 2.4 %fusion.9 = f32[128,4096]{1,0:T(8,128)S(1)} fusion(bf16[2048,4096]{1,0:T(8,128)(2,1)S(1)} %copy-done.3, bf16[128,8192]{1,0:T(8,128)(2,1)S(1)} %fusion.2), kind=kOutput, calls=%fused_computation.18 | convolution fusion | flops 2147483648 | bytes 19398656 | tf_op jit(solution)/shard_map/dot_general | solution.py:40
  20.7 1.4 %fusion.8 = (f32[128]{0:T(128)S(1)}, f32[128,2048]{1,0:T(8,128)S(1)}, f32[128,2048]{1,0:T(8,128)S(1)}) fusion(pred[2048]{0:T(1024)(128)(4,1)S(1)} %get-tuple-element.10, f32[128,4096]{1,0:T(8,128)S(1)} %fusion.9, pred[2048]{0:T(1024)(128)(4,1)S(1)} %get-tuple-element.13, pred[2048]{0:T(1024)(128)(4,1)S(1)} %broadcast_compare_fusion.8, ...), kind=kLoop, calls=%fused_computation.17 | loop fusion | flops 9174912 | bytes 10504704 | tf_op jit(solution)/shard_map/reduce_sum | solution.py:57
  22.2 0.0 copy-start
  22.2 0.0 copy-start.1
  22.2 0.0 copy-start.2
  22.2 0.6 multiply_convert_fusion.1
  22.8 0.1 pad_maximum_fusion.white
  22.9 0.9 %convert_multiply_fusion.weights = f32[2,64,256]{2,1,0:T(8,128)S(1)} fusion(s32[2,256,256]{2,1,0:T(8,128)} %param.8, s32[]{:T(128)S(6)} %select_n.168), kind=kLoop, calls=%fused_computation.26 | loop fusion | flops 65536 | bytes 262148 | tf_op jit(solution)/shard_map/mul | solution.py:277
  23.8 0.0 copy-done
  23.8 0.0 copy-done.1
  23.8 0.0 copy-done.2
  23.8 58.6 %shard_map.64 = f32[2,64,1024]{2,1,0:T(8,128)S(1)} custom-call(bf16[128,4096]{1,0:T(8,128)(2,1)S(1)} %pad_maximum_fusion.white, s32[2,2]{1,0:T(2,128)S(1)} %copy-done, f32[2,64,256]{2,1,0:T(8,128)S(1)} %convert_multiply_fusion.weights, f32[4,2048]{1,0:T(4,128)S(1)} %copy-done.1, f32[4,2048]{1,0:T(4,128)S(1)} %copy-done.2), custom_call_target="tpu_custom_call" | custom-call | flops 5000000000 | bytes 4000000 | tf_op jit(solution)/shard_map/pallas_call | solution.py:282
  82.4 0.8 copy.8
  (7 shorter events, 0.1 us)
Async XLA Ops:
  0.0 2.2 %copy-start.4 = (bf16[1,128,8192]{2,1,0:T(8,128)(2,1)S(1)}, bf16[1,128,8192]{2,1,0:T(8,128)(2,1)}, u32[]{:S(2)}) copy-start(bf16[1,128,8192]{2,1,0:T(8,128)(2,1)} %param.6) | copy-start | bytes 6291460
  2.9 10.5 %copy-start.3 = (bf16[2048,4096]{1,0:T(8,128)(2,1)S(1)}, bf16[2048,4096]{1,0:T(8,128)(2,1)}, u32[]{:S(2)}) copy-start(bf16[2048,4096]{1,0:T(8,128)(2,1)} %constant.84.clone) | copy-start | bytes 50331652
  22.2 1.6 %copy-start = (s32[2,2]{1,0:T(2,128)S(1)}, s32[2,2]{1,0:T(2,128)}, u32[]{:S(2)}) copy-start(s32[2,2]{1,0:T(2,128)} %pairs.1) | copy-start | bytes 52
  22.2 1.6 %copy-start.1 = (f32[4,2048]{1,0:T(4,128)S(1)}, f32[4,2048]{1,0:T(4,128)}, u32[]{:S(2)}) copy-start(f32[4,2048]{1,0:T(4,128)} %constant.85.clone.cosines) | copy-start | bytes 98308
  22.2 1.6 %copy-start.2 = (f32[4,2048]{1,0:T(4,128)S(1)}, f32[4,2048]{1,0:T(4,128)}, u32[]{:S(2)}) copy-start(f32[4,2048]{1,0:T(4,128)} %constant.86.clone.sines) | copy-start | bytes 98308

commit v3 on v2

--- a/solution.py
+++ b/solution.py
@@ -18,51 +18,94 @@
 LAG_STEP = 25
 
 
+BINS = 256
+ORDER = np.argsort((F_LO + np.arange(F)) % 4, kind="stable")
+FREQS = F_LO + ORDER
+
+
 def quarter_table():
-    phase = (np.arange(NT // 4)[:, None] * (F_LO + np.arange(F))[None, :]) % NT
-    angle = phase * (2.0 * math.pi / NT)
-    return np.concatenate([np.cos(angle), np.sin(angle)], axis=1).astype(ml_dtypes.bfloat16)
-
-
-def transform(rows):
-    values = rows.astype(jnp.float32)
-    values = values - jnp.mean(values, axis=-1, keepdims=True)
-    times = jnp.arange(NT).astype(jnp.float32)
-    window = 0.5 - 0.5 * jnp.cos(times * (2.0 * math.pi / NT))
-    tapered = (values * window).astype(jnp.bfloat16)
-    quarter = NT // 4
-    freqs = F_LO + jnp.arange(F)
-    table = jnp.asarray(quarter_table())
-    real_total = jnp.zeros((rows.shape[0], F), jnp.float32)
-    imag_total = jnp.zeros((rows.shape[0], F), jnp.float32)
-    for quarter_index in range(4):
-        part_rows = tapered[:, quarter_index * quarter : (quarter_index + 1) * quarter]
-        product = jnp.dot(part_rows, table, preferred_element_type=jnp.float32)
-        cos_part = product[:, :F]
-        sin_part = product[:, F:]
-        turns = jnp.mod(quarter_index * freqs, 4)[None, :]
-        real_add = jnp.where(
-            turns == 0,
-            cos_part,
-            jnp.where(turns == 1, -sin_part, jnp.where(turns == 2, -cos_part, sin_part)),
-        )
-        imag_add = jnp.where(
-            turns == 0,
-            -sin_part,
-            jnp.where(turns == 1, -cos_part, jnp.where(turns == 2, sin_part, cos_part)),
-        )
-        real_total = real_total + real_add
-        imag_total = imag_total + imag_add
-    power = real_total * real_total + imag_total * imag_total
-    level = jnp.mean(power, axis=-1, keepdims=True)
-    scale = 1.0 / jnp.sqrt(power + 0.01 * level + 1e-06)
-    return jnp.concatenate([real_total * scale, imag_total * scale], axis=-1).astype(jnp.bfloat16)
+    phase = (np.arange(NT // 4)[:, None] * FREQS[None, :]) % NT
+    angle = (phase * (2.0 * math.pi / NT)).reshape(NT // 4, F // BINS, 1, BINS)
+    both = np.concatenate([np.cos(angle), np.sin(angle)], axis=2)
+    return both.transpose(1, 0, 2, 3).reshape(F // BINS, NT // 4, 2 * BINS).astype(ml_dtypes.bfloat16)
 
 
 def lag_tables():
     lags = (np.arange(LAGS) - LAGS // 2) * LAG_STEP
-    phase = ((lags[:, None] * (F_LO + np.arange(F))[None, :]) % NT) * (2.0 * math.pi / NT)
+    phase = ((lags[:, None] * FREQS[None, :]) % NT) * (2.0 * math.pi / NT)
     return np.cos(phase).astype(np.float32), np.sin(phase).astype(np.float32)
+
+
+def transform_kernel(signal, window, table, white, tapered, spectrum, power_sum):
+    rows = signal.shape[1]
+    quarter = NT // 4
+    step = pl.program_id(0)
+
+    @pl.when(step == 0)
+    def _():
+        total = jnp.zeros((rows, 1), jnp.float32)
+        for part in range(4):
+            values = signal[0, :, part * quarter : (part + 1) * quarter].astype(jnp.float32)
+            total = total + jnp.sum(values, axis=-1, keepdims=True)
+        mean = total / NT
+        for part in range(4):
+            cols = pl.ds(part * quarter, quarter)
+            values = (signal[0, :, cols].astype(jnp.float32) - mean) * window[:, cols]
+            tapered[pl.ds(part * rows, rows), :] = values.astype(jnp.bfloat16)
+        power_sum[...] = jnp.zeros_like(power_sum)
+
+    product = jnp.dot(tapered[...], table[0], preferred_element_type=jnp.float32)
+    residue = step // (F // 4 // BINS)
+    real_total = product[:rows, :BINS]
+    imag_total = -product[:rows, BINS:]
+    for part in range(1, 4):
+        cos_part = product[part * rows : (part + 1) * rows, :BINS]
+        sin_part = product[part * rows : (part + 1) * rows, BINS:]
+        turn = (part * residue) % 4
+        c = jnp.where(turn == 0, 1.0, jnp.where(turn == 2, -1.0, 0.0))
+        d = jnp.where(turn == 1, -1.0, jnp.where(turn == 3, 1.0, 0.0))
+        real_total = real_total + (c * cos_part + d * sin_part)
+        imag_total = imag_total + (d * cos_part - c * sin_part)
+    start = pl.multiple_of(step * BINS, BINS)
+    spectrum[:, pl.ds(start, BINS)] = real_total
+    spectrum[:, pl.ds(F + start, BINS)] = imag_total
+    power = real_total * real_total + imag_total * imag_total
+    power_sum[...] += jnp.sum(power, axis=-1, keepdims=True)
+
+    @pl.when(step == F // BINS - 1)
+    def _():
+        floor = 0.01 * (power_sum[...] / F) + 1e-06
+        for part in range(F // 512):
+            real_cols = pl.ds(part * 512, 512)
+            imag_cols = pl.ds(F + part * 512, 512)
+            real_part = spectrum[:, real_cols]
+            imag_part = spectrum[:, imag_cols]
+            scale = lax.rsqrt(real_part * real_part + imag_part * imag_part + floor)
+            white[:, real_cols] = (real_part * scale).astype(jnp.bfloat16)
+            white[:, imag_cols] = (imag_part * scale).astype(jnp.bfloat16)
+
+
+def transform(signal):
+    rows = signal.shape[1]
+    window = (0.5 - 0.5 * np.cos(np.arange(NT) * (2.0 * math.pi / NT))).astype(np.float32)[None]
+    return pl.pallas_call(
+        transform_kernel,
+        grid=(F // BINS,),
+        out_shape=jax.ShapeDtypeStruct((rows, 2 * F), jnp.bfloat16),
+        in_specs=[
+            pl.BlockSpec((1, rows, NT), lambda step: (0, 0, 0)),
+            pl.BlockSpec((1, NT), lambda step: (0, 0)),
+            pl.BlockSpec((1, NT // 4, 2 * BINS), lambda step: (step, 0, 0)),
+        ],
+        out_specs=pl.BlockSpec((rows, 2 * F), lambda step: (0, 0)),
+        scratch_shapes=[
+            pltpu.VMEM((4 * rows, NT // 4), jnp.bfloat16),
+            pltpu.VMEM((rows, 2 * F), jnp.float32),
+            pltpu.VMEM((rows, 1), jnp.float32),
+        ],
+        compiler_params=pltpu.CompilerParams(vmem_limit_bytes=40 * 1024 * 1024),
+        cost_estimate=pl.CostEstimate(flops=9 * 10**9, bytes_accessed=20 * 10**6, transcendentals=0),
+    )(signal, window, quarter_table())
 
 
 def correlate_kernel(
@@ -265,7 +308,7 @@
 
 
 def shards(signal, tile_list, band_mask):
-    white = transform(signal[0])
+    white = transform(signal)
     slot_count = tile_list.shape[0]
     windows = lax.axis_size("win")
     half = white.shape[0]

time: 83.4 us -> 77.7 us (0.932)
  matrix products: 15.5 us -> 0 us
  Pallas kernels: 58.6 us -> 73.1 us
  other arithmetic: 5.9 us -> 0.96 us
    dot_general x4 -> x0, matrix products: 15.5 us -> none  [transform(): product = jnp.dot(part_rows, table, preferred_element_type=jnp.float32)]
    pallas_call x0 -> x1, Pallas kernels: none -> 14.5 us  [transform(): pl.pallas_call(transform_kernel, grid=(F // BINS,), out_shape=jax.ShapeDt...]
    reduce_sum x2 -> x0, other arithmetic: 3.48 us -> none  [the longest x1 2.07 us: transform(): values = values - jnp.mean(values, axis=-1, keepdims=True)]
where the time goes in v3:
time: 77.7 us; the launch traced here: 77.3 us
  Pallas kernels  73.1 us (94%)
  local copies, waits for them, and re-layouts  3.15 us (4%)
  other arithmetic  0.96 us (1%)
    pallas_call x1, Pallas kernels, shards(): pl.pallas_call(functools.partial(correlate_kernel, blocks, windows), out_...  58.6 us
    pallas_call x1, Pallas kernels, transform(): pl.pallas_call(transform_kernel, grid=(F // BINS,), out_shape=jax.ShapeDt...  14.5 us
    unnamed x11, local copies, waits for them, and re-layouts  3.15 us

profile of v3, /device:TPU:15, one launch (start us, length us, event | category | flops | bytes accessed | tf_op | source)
XLA Modules:
  0.0 77.3 jit_solution(4611888601150162873)
XLA Ops:
  0.0 0.0 copy-start.1
  0.0 0.0 copy-start.2
  0.0 0.0 copy-start.3
  0.0 1.0 %convert_multiply_fusion.weights = f32[2,64,256]{2,1,0:T(8,128)S(1)} fusion(s32[2,256,256]{2,1,0:T(8,128)} %param.9, s32[]{:T(128)S(6)} %select_n.3), kind=kLoop, calls=%fused_computation | loop fusion | flops 65536 | bytes 262148 | tf_op jit(solution)/shard_map/mul | solution.py:320
  1.0 0.0 copy-start
  1.0 1.6 %copy-done = bf16[1,128,8192]{2,1,0:T(8,128)(2,1)S(1)} copy-done((bf16[1,128,8192]{2,1,0:T(8,128)(2,1)S(1)}, bf16[1,128,8192]{2,1,0:T(8,128)(2,1)}, u32[]{:S(2)}) %copy-start) | copy-done | bytes 2097176
  2.6 0.0 copy-start.4
  2.6 0.8 copy-done.4
  3.3 14.5 %shard_map.73.white = bf16[128,4096]{1,0:T(8,128)(2,1)S(1)} custom-call(bf16[1,128,8192]{2,1,0:T(8,128)(2,1)S(1)} %copy-done, f32[1,8192]{1,0:T(1,128)S(1)} %copy-done.4, bf16[8,2048,512]{2,1,0:T(8,128)(2,1)} %constant.21.clone.table), custom_call_target="tpu_custom_call" | custom-call | flops 8999999488 | bytes 20000000 | tf_op jit(solution)/shard_map/pallas_call | solution.py:91
  17.9 0.0 copy-done.1
  17.9 0.0 copy-done.2
  17.9 0.0 copy-done.3
  17.9 58.6 %shard_map.74 = f32[2,64,1024]{2,1,0:T(8,128)S(1)} custom-call(bf16[128,4096]{1,0:T(8,128)(2,1)S(1)} %shard_map.73.white, s32[2,2]{1,0:T(2,128)S(1)} %copy-done.1, f32[2,64,256]{2,1,0:T(8,128)S(1)} %convert_multiply_fusion.weights, f32[4,2048]{1,0:T(4,128)S(1)} %copy-done.3, f32[4,2048]{1,0:T(4,128)S(1)} %copy-done.2), custom_call_target="tpu_custom_call" | custom-call | flops 5000000000 | bytes 4000000 | tf_op jit(solution)/shard_map/pallas_call | solution.py:325
  76.5 0.8 %copy.9 = f32[2,64,1024]{2,1,0:T(8,128)} copy(f32[2,64,1024]{2,1,0:T(8,128)S(1)} %shard_map.74) | data formatting | bytes 1048576
Async XLA Ops:
  0.0 17.9 %copy-start.1 = (s32[2,2]{1,0:T(2,128)S(1)}, s32[2,2]{1,0:T(2,128)}, u32[]{:S(2)}) copy-start(s32[2,2]{1,0:T(2,128)} %pairs.1) | copy-start | bytes 52
  0.0 17.9 %copy-start.2 = (f32[4,2048]{1,0:T(4,128)S(1)}, f32[4,2048]{1,0:T(4,128)}, u32[]{:S(2)}) copy-start(f32[4,2048]{1,0:T(4,128)} %constant.23.clone.sines) | copy-start | bytes 98308
  0.0 17.9 %copy-start.3 = (f32[4,2048]{1,0:T(4,128)S(1)}, f32[4,2048]{1,0:T(4,128)}, u32[]{:S(2)}) copy-start(f32[4,2048]{1,0:T(4,128)} %constant.22.clone.cosines) | copy-start | bytes 98308
  1.0 1.6 %copy-start = (bf16[1,128,8192]{2,1,0:T(8,128)(2,1)S(1)}, bf16[1,128,8192]{2,1,0:T(8,128)(2,1)}, u32[]{:S(2)}) copy-start(bf16[1,128,8192]{2,1,0:T(8,128)(2,1)} %signal.1) | copy-start | bytes 6291460
  2.6 0.8 copy-start.4

commit v4 on v3

--- a/solution.py
+++ b/solution.py
@@ -103,7 +103,7 @@
             pltpu.VMEM((rows, 2 * F), jnp.float32),
             pltpu.VMEM((rows, 1), jnp.float32),
         ],
-        compiler_params=pltpu.CompilerParams(vmem_limit_bytes=40 * 1024 * 1024),
+        compiler_params=pltpu.CompilerParams(vmem_limit_bytes=56 * 1024 * 1024),
         cost_estimate=pl.CostEstimate(flops=9 * 10**9, bytes_accessed=20 * 10**6, transcendentals=0),
     )(signal, window, quarter_table())
 
@@ -112,7 +112,7 @@
     blocks, windows,
     white, pairs, weights, cosines, sines,
     out,
-    left, left_next, right_far, rotated, product, outgoing, incoming, own_rows, gathered,
+    left, left_next, right_near, right_far, rotated, product, outgoing, incoming, own_rows, gathered,
     half_send, half_recv, local_sem, win_send, win_recv, tile_send, tile_recv, pass_send, pass_recv,
 ):
     half = white.shape[0]
@@ -126,10 +126,11 @@
     def holds(which):
         even = which % 2 == 0
         far = which + 2 < blocks
-        return [which >= 0, even, far, jnp.logical_and(even, far)]
+        across = jnp.logical_and(which % 2 == 1, which >= 3)
+        return [which >= 0, even, far, across]
 
     mine = holds(chip)
-    even, far = mine[1], mine[2]
+    even, far, across = mine[1], mine[2], mine[3]
 
     def remote(src, dst, send, recv, **where):
         return pltpu.make_async_remote_copy(
@@ -152,20 +153,24 @@
         )
     pl.semaphore_wait(barrier, blocks + windows - 1)
 
-    odd_chip = chip % 2 == 1
-    late_chip = chip >= 2
-    before = lax.rem(chip + blocks - 1, blocks) * 2 + core
-    before2 = lax.rem(chip + blocks - 2, blocks) * 2 + core
-    to_before = remote(white, left_next.at[my_half], half_send.at[0], half_recv.at[0], tile=before)
-    to_before2 = remote(white, right_far, half_send.at[1], half_recv.at[1], tile=before2)
+    sends_near = chip >= 1
+    sends_far = chip >= 2
+    sends_left = jnp.logical_and(chip % 2 == 1, far)
+    partner = lax.rem(chip + 1 - 2 * (chip % 2) + blocks, blocks) * 2 + core
+    to_near = remote(white, right_near, half_send.at[0], half_recv.at[0], tile=partner)
+    to_far = remote(white, right_far, half_send.at[1], half_recv.at[1], tile=chip_ahead(blocks - 2) * 2 + core)
+    to_left = remote(
+        white, left_next.at[my_half], half_send.at[4], half_recv.at[4], tile=chip_ahead(2) * 2 + core
+    )
     to_sibling = remote(white, left.at[my_half], half_send.at[2], half_recv.at[2], tile=sibling)
     pass_on = remote(
         left_next.at[my_half], left_next.at[my_half], half_send.at[3], half_recv.at[3], tile=sibling
     )
     keep = pltpu.make_async_copy(white, left.at[my_half], local_sem)
 
-    pl.when(odd_chip)(to_before.start)
-    pl.when(late_chip)(to_before2.start)
+    pl.when(sends_near)(to_near.start)
+    pl.when(sends_far)(to_far.start)
+    pl.when(sends_left)(to_left.start)
     to_sibling.start()
     keep.start()
 
@@ -232,27 +237,27 @@
     to_sibling.wait_recv()
     multiply(0, left)
 
+    collect(0)
+
     @pl.when(even)
     def _():
-        to_before.wait_recv()
-        pass_on.start()
-        rotate(lambda cols: left_next[my_half, cols])
+        to_near.wait_recv()
+        rotate(lambda cols: right_near[:, cols])
         multiply(1, left)
 
-    collect(0)
-
     @pl.when(far)
     def _():
-        to_before2.wait_recv()
+        to_far.wait_recv()
         rotate(lambda cols: right_far[:, cols])
         multiply(2, left)
 
-    @pl.when(even)
-    def _():
+    @pl.when(across)
+    def _():
+        to_left.wait_recv()
+        pass_on.start()
+        to_near.wait_recv()
+        rotate(lambda cols: right_near[:, cols])
         pass_on.wait_recv()
-
-    @pl.when(mine[3])
-    def _():
         multiply(3, left_next)
 
     for t in range(1, 4):
@@ -279,7 +284,7 @@
         live = row_block >= 0
         row_block = jnp.maximum(row_block, 0)
         step_in = jnp.logical_and(distance == 1, row_block % 2 == 1)
-        place = jnp.where(step_in, row_block - 1, row_block)
+        place = jnp.where(step_in, row_block + 2, row_block)
         which = jnp.where(step_in, 3, distance)
         for side in range(2):
             values = gathered[side, place, which]
@@ -289,10 +294,11 @@
                 piece = values[:, k * half : (k + 1) * half] * factor
                 out[slot, :, pl.ds(k * CB + side * half, half)] = jnp.where(live, piece, 0.0)
 
-    pl.when(odd_chip)(to_before.wait_send)
-    pl.when(late_chip)(to_before2.wait_send)
+    pl.when(sends_near)(to_near.wait_send)
+    pl.when(sends_far)(to_far.wait_send)
+    pl.when(sends_left)(to_left.wait_send)
     to_sibling.wait_send()
-    pl.when(even)(pass_on.wait_send)
+    pl.when(across)(pass_on.wait_send)
 
     for t in range(4):
 
@@ -331,13 +337,14 @@
             pltpu.VMEM((CB, 2 * F), jnp.bfloat16),
             pltpu.VMEM((CB, 2 * F), jnp.bfloat16),
             pltpu.VMEM((half, 2 * F), jnp.bfloat16),
+            pltpu.VMEM((half, 2 * F), jnp.bfloat16),
             pltpu.VMEM((width, 2 * F), jnp.bfloat16),
             pltpu.VMEM((CB, width), jnp.float32),
             pltpu.VMEM((4, CB, width), jnp.bfloat16),
             pltpu.VMEM((4, windows - 1, rows_here, width), jnp.bfloat16),
             pltpu.VMEM((4, rows_here, width), jnp.float32),
             pltpu.VMEM((2, blocks, 4, rows_here, width), jnp.float32),
-            dma((4,)), dma((4,)), dma,
+            dma((5,)), dma((5,)), dma,
             dma((4, windows - 1)), dma((4, windows - 1)),
             dma((4, blocks - 1)), dma((4, blocks - 1)),
             dma((4, blocks)), dma((4, blocks)),

time: 77.7 us -> 71 us (0.914)
  Pallas kernels: 73.1 us -> 67.7 us
  local copies, waits for them, and re-layouts: 3.15 us -> 2.02 us
    pallas_call x1, Pallas kernels: 58.6 us -> 51.6 us  [shards(): pl.pallas_call(functools.partial(correlate_kernel, blocks, windows), out_...]
    pallas_call x1, Pallas kernels: 14.5 us -> 16.1 us  [transform(): pl.pallas_call(transform_kernel, grid=(F // BINS,), out_shape=jax.ShapeDt...]
    unnamed x11 -> x9, local copies, waits for them, and re-layouts: 3.15 us -> 2.02 us
where the time goes in v4:
time: 71 us; the launch traced here: 70.7 us
  Pallas kernels  67.7 us (95%)
  local copies, waits for them, and re-layouts  2.02 us (3%)
  other arithmetic  0.96 us (1%)
    pallas_call x1, Pallas kernels, shards(): pl.pallas_call(functools.partial(correlate_kernel, blocks, windows), out_...  51.6 us
    pallas_call x1, Pallas kernels, transform(): pl.pallas_call(transform_kernel, grid=(F // BINS,), out_shape=jax.ShapeDt...  16.1 us
    unnamed x9, local copies, waits for them, and re-layouts  2.02 us

profile of v4, /device:TPU:15, one launch (start us, length us, event | category | flops | bytes accessed | tf_op | source)
XLA Modules:
  0.0 70.7 jit_solution(3839656172240789797)
XLA Ops:
  0.0 0.0 copy-start
  0.0 0.0 copy-start.1
  0.0 0.0 copy-start.2
  0.0 1.0 %convert_multiply_fusion.weights = f32[2,64,256]{2,1,0:T(8,128)S(1)} fusion(s32[2,256,256]{2,1,0:T(8,128)} %param.9, s32[]{:T(128)S(6)} %select_n.3), kind=kLoop, calls=%fused_computation | loop fusion | flops 65536 | bytes 262148 | tf_op jit(solution)/shard_map/mul | solution.py:326
  1.0 16.1 %shard_map.73.white = bf16[128,4096]{1,0:T(8,128)(2,1)} custom-call(bf16[1,128,8192]{2,1,0:T(8,128)(2,1)} %signal.1, f32[1,8192]{1,0:T(1,128)} %constant.20.clone.window, bf16[8,2048,512]{2,1,0:T(8,128)(2,1)} %constant.21.clone.table), custom_call_target="tpu_custom_call" | custom-call | flops 8999999488 | bytes 20000000 | tf_op jit(solution)/shard_map/pallas_call | solution.py:91
  17.1 0.0 copy-done
  17.1 0.0 copy-done.1
  17.1 0.0 copy-done.2
  17.1 0.0 copy-start.3
  17.1 1.2 %copy-done.3 = bf16[128,4096]{1,0:T(8,128)(2,1)S(1)} copy-done((bf16[128,4096]{1,0:T(8,128)(2,1)S(1)}, bf16[128,4096]{1,0:T(8,128)(2,1)}, u32[]{:S(2)}) %copy-start.3) | copy-done | bytes 1048600
  18.3 51.6 %shard_map.74 = f32[2,64,1024]{2,1,0:T(8,128)S(1)} custom-call(bf16[128,4096]{1,0:T(8,128)(2,1)S(1)} %copy-done.3, s32[2,2]{1,0:T(2,128)S(1)} %copy-done, f32[2,64,256]{2,1,0:T(8,128)S(1)} %convert_multiply_fusion.weights, f32[4,2048]{1,0:T(4,128)S(1)} %copy-done.2, f32[4,2048]{1,0:T(4,128)S(1)} %copy-done.1), custom_call_target="tpu_custom_call" | custom-call | flops 5000000000 | bytes 4000000 | tf_op jit(solution)/shard_map/pallas_call | solution.py:331
  69.9 0.8 %copy.9 = f32[2,64,1024]{2,1,0:T(8,128)} copy(f32[2,64,1024]{2,1,0:T(8,128)S(1)} %shard_map.74) | data formatting | bytes 1048576
Async XLA Ops:
  0.0 17.1 %copy-start = (s32[2,2]{1,0:T(2,128)S(1)}, s32[2,2]{1,0:T(2,128)}, u32[]{:S(2)}) copy-start(s32[2,2]{1,0:T(2,128)} %pairs.1) | copy-start | bytes 52
  0.0 17.1 %copy-start.1 = (f32[4,2048]{1,0:T(4,128)S(1)}, f32[4,2048]{1,0:T(4,128)}, u32[]{:S(2)}) copy-start(f32[4,2048]{1,0:T(4,128)} %constant.23.clone.sines) | copy-start | bytes 98308
  0.0 17.1 %copy-start.2 = (f32[4,2048]{1,0:T(4,128)S(1)}, f32[4,2048]{1,0:T(4,128)}, u32[]{:S(2)}) copy-start(f32[4,2048]{1,0:T(4,128)} %constant.22.clone.cosines) | copy-start | bytes 98308
  17.1 1.2 %copy-start.3 = (bf16[128,4096]{1,0:T(8,128)(2,1)S(1)}, bf16[128,4096]{1,0:T(8,128)(2,1)}, u32[]{:S(2)}) copy-start(bf16[128,4096]{1,0:T(8,128)(2,1)} %shard_map.73.white) | copy-start | bytes 3145732

commit v5 on v4

--- a/solution.py
+++ b/solution.py
@@ -19,6 +19,7 @@
 
 
 BINS = 256
+PIECES = 2
 ORDER = np.argsort((F_LO + np.arange(F)) % 4, kind="stable")
 FREQS = F_LO + ORDER
 
@@ -121,16 +122,17 @@
     win = lax.axis_index("win")
     chip, core = tile // 2, tile % 2
     sibling = chip * 2 + (1 - core)
+    few = half // PIECES
     my_half = pl.ds(pl.multiple_of(core * half, half), half)
 
     def holds(which):
         even = which % 2 == 0
         far = which + 2 < blocks
         across = jnp.logical_and(which % 2 == 1, which >= 3)
-        return [which >= 0, even, far, across]
+        return [tile_here for tile_here in (which >= 0, even, far, across) for _ in range(PIECES)]
 
     mine = holds(chip)
-    even, far, across = mine[1], mine[2], mine[3]
+    even, far, across = mine[PIECES], mine[2 * PIECES], mine[3 * PIECES]
 
     def remote(src, dst, send, recv, **where):
         return pltpu.make_async_remote_copy(
@@ -157,34 +159,47 @@
     sends_far = chip >= 2
     sends_left = jnp.logical_and(chip % 2 == 1, far)
     partner = lax.rem(chip + 1 - 2 * (chip % 2) + blocks, blocks) * 2 + core
-    to_near = remote(white, right_near, half_send.at[0], half_recv.at[0], tile=partner)
-    to_far = remote(white, right_far, half_send.at[1], half_recv.at[1], tile=chip_ahead(blocks - 2) * 2 + core)
+    to_near, to_far = [], []
+    for piece in range(PIECES):
+        rows = pl.ds(piece * few, few)
+        near_at, far_at = 3 + 2 * piece, 4 + 2 * piece
+        to_near.append(
+            remote(white.at[rows], right_near.at[rows], half_send.at[near_at], half_recv.at[near_at], tile=partner)
+        )
+        to_far.append(
+            remote(
+                white.at[rows], right_far.at[rows], half_send.at[far_at], half_recv.at[far_at],
+                tile=chip_ahead(blocks - 2) * 2 + core,
+            )
+        )
     to_left = remote(
-        white, left_next.at[my_half], half_send.at[4], half_recv.at[4], tile=chip_ahead(2) * 2 + core
+        white, left_next.at[my_half], half_send.at[0], half_recv.at[0], tile=chip_ahead(2) * 2 + core
     )
     to_sibling = remote(white, left.at[my_half], half_send.at[2], half_recv.at[2], tile=sibling)
     pass_on = remote(
-        left_next.at[my_half], left_next.at[my_half], half_send.at[3], half_recv.at[3], tile=sibling
+        left_next.at[my_half], left_next.at[my_half], half_send.at[1], half_recv.at[1], tile=sibling
     )
     keep = pltpu.make_async_copy(white, left.at[my_half], local_sem)
 
-    pl.when(sends_near)(to_near.start)
-    pl.when(sends_far)(to_far.start)
+    for piece in range(PIECES):
+        pl.when(sends_near)(to_near[piece].start)
+        pl.when(sends_far)(to_far[piece].start)
     pl.when(sends_left)(to_left.start)
     to_sibling.start()
     keep.start()
 
-    def rotate(read):
-        width = 512
-        for part in range(F // width):
-            real_cols = pl.ds(part * width, width)
-            imag_cols = pl.ds(F + part * width, width)
-            real_part = read(real_cols).astype(jnp.float32)
-            imag_part = read(imag_cols).astype(jnp.float32)
+    def rotate(right, piece):
+        chunk = 512
+        rows = pl.ds(piece * few, few)
+        for part in range(F // chunk):
+            real_cols = pl.ds(part * chunk, chunk)
+            imag_cols = pl.ds(F + part * chunk, chunk)
+            real_part = right[rows, real_cols].astype(jnp.float32)
+            imag_part = right[rows, imag_cols].astype(jnp.float32)
             for k in range(LAGS):
                 c = cosines[pl.ds(k, 1), real_cols]
                 s = sines[pl.ds(k, 1), real_cols]
-                lag_rows = pl.ds(k * half, half)
+                lag_rows = pl.ds(k * few, few)
                 rotated[lag_rows, real_cols] = (real_part * c + imag_part * s).astype(jnp.bfloat16)
                 rotated[lag_rows, imag_cols] = (imag_part * c - real_part * s).astype(jnp.bfloat16)
 
@@ -200,12 +215,9 @@
         return 1.0 + index.astype(jnp.float32) / windows
 
     def multiply(t, rows_ref):
-        for part in range(LAGS * half // 256):
-            cols = pl.ds(part * 256, 256)
-            product[:, cols] = lax.dot_general(
-                rows_ref[...], rotated[cols, :], (((1,), (1,)), ((), ())),
-                preferred_element_type=jnp.float32,
-            )
+        product[...] = lax.dot_general(
+            rows_ref[...], rotated[...], (((1,), (1,)), ((), ())), preferred_element_type=jnp.float32
+        )
         outgoing[t] = (product[...] * spread(win)).astype(jnp.bfloat16)
         own_rows[t] = product[pl.ds(pl.multiple_of(win * rows_here, rows_here), rows_here), :]
         for step in range(1, windows):
@@ -233,37 +245,45 @@
         pass_copy(t, 0).start()
 
     keep.wait()
-    rotate(lambda cols: white[:, cols])
-    to_sibling.wait_recv()
-    multiply(0, left)
-
-    collect(0)
-
-    @pl.when(even)
-    def _():
-        to_near.wait_recv()
-        rotate(lambda cols: right_near[:, cols])
-        multiply(1, left)
-
-    @pl.when(far)
-    def _():
-        to_far.wait_recv()
-        rotate(lambda cols: right_far[:, cols])
-        multiply(2, left)
-
-    @pl.when(across)
-    def _():
-        to_left.wait_recv()
-        pass_on.start()
-        to_near.wait_recv()
-        rotate(lambda cols: right_near[:, cols])
-        pass_on.wait_recv()
-        multiply(3, left_next)
-
-    for t in range(1, 4):
+    for piece in range(PIECES):
+        rotate(white, piece)
+        if piece == 0:
+            to_sibling.wait_recv()
+        multiply(piece, left)
+
+    for piece in range(PIECES):
+
+        @pl.when(even)
+        def _():
+            to_near[piece].wait_recv()
+            rotate(right_near, piece)
+            multiply(PIECES + piece, left)
+
+        @pl.when(far)
+        def _():
+            to_far[piece].wait_recv()
+            rotate(right_far, piece)
+            multiply(2 * PIECES + piece, left)
+
+        @pl.when(across)
+        def _():
+            if piece == 0:
+                to_left.wait_recv()
+                pass_on.start()
+            to_near[piece].wait_recv()
+            rotate(right_near, piece)
+            if piece == 0:
+                pass_on.wait_recv()
+            multiply(3 * PIECES + piece, left_next)
+
+        if piece == 0:
+            for t in range(PIECES):
+                collect(t)
+
+    for t in [tile_kind * PIECES + piece for piece in range(PIECES) for tile_kind in range(1, 4)]:
         pl.when(mine[t])(functools.partial(collect, t))
 
-    for t in range(4):
+    for t in [tile_kind * PIECES + piece for piece in range(PIECES) for tile_kind in range(4)]:
         for step in range(1, blocks):
 
             @pl.when(holds(chip_ahead(blocks - step))[t])
@@ -271,7 +291,7 @@
                 tile_copy(t, step).wait_recv()
                 pass_copy(t, step).start()
 
-    for t in range(4):
+    for t in [tile_kind * PIECES + piece for piece in range(PIECES) for tile_kind in range(4)]:
         for step in range(blocks):
 
             @pl.when(holds(chip_ahead(blocks - step))[t])
@@ -287,20 +307,21 @@
         place = jnp.where(step_in, row_block + 2, row_block)
         which = jnp.where(step_in, 3, distance)
         for side in range(2):
-            values = gathered[side, place, which]
+            values = [gathered[side, place, which * PIECES + piece] for piece in range(PIECES)]
             side_cols = pl.ds(side * half, half)
             factor = weights[slot, :, side_cols]
             for k in range(LAGS):
-                piece = values[:, k * half : (k + 1) * half] * factor
-                out[slot, :, pl.ds(k * CB + side * half, half)] = jnp.where(live, piece, 0.0)
-
-    pl.when(sends_near)(to_near.wait_send)
-    pl.when(sends_far)(to_far.wait_send)
+                lag = jnp.concatenate([value[:, k * few : (k + 1) * few] for value in values], axis=1)
+                out[slot, :, pl.ds(k * CB + side * half, half)] = jnp.where(live, lag * factor, 0.0)
+
+    for piece in range(PIECES):
+        pl.when(sends_near)(to_near[piece].wait_send)
+        pl.when(sends_far)(to_far[piece].wait_send)
     pl.when(sends_left)(to_left.wait_send)
     to_sibling.wait_send()
     pl.when(across)(pass_on.wait_send)
 
-    for t in range(4):
+    for t in [tile_kind * PIECES + piece for piece in range(PIECES) for tile_kind in range(4)]:
 
         @pl.when(mine[t])
         def _():
@@ -327,7 +348,8 @@
     cosines, sines = lag_tables()
     vmem = pl.BlockSpec(memory_space=pltpu.VMEM)
     dma = pltpu.SemaphoreType.DMA
-    width = LAGS * half
+    width = LAGS * half // PIECES
+    units = 4 * PIECES
     return pl.pallas_call(
         functools.partial(correlate_kernel, blocks, windows),
         out_shape=jax.ShapeDtypeStruct((slot_count, rows_here, LAGS * CB), jnp.float32),
@@ -340,14 +362,14 @@
             pltpu.VMEM((half, 2 * F), jnp.bfloat16),
             pltpu.VMEM((width, 2 * F), jnp.bfloat16),
             pltpu.VMEM((CB, width), jnp.float32),
-            pltpu.VMEM((4, CB, width), jnp.bfloat16),
-            pltpu.VMEM((4, windows - 1, rows_here, width), jnp.bfloat16),
-            pltpu.VMEM((4, rows_here, width), jnp.float32),
-            pltpu.VMEM((2, blocks, 4, rows_here, width), jnp.float32),
-            dma((5,)), dma((5,)), dma,
-            dma((4, windows - 1)), dma((4, windows - 1)),
-            dma((4, blocks - 1)), dma((4, blocks - 1)),
-            dma((4, blocks)), dma((4, blocks)),
+            pltpu.VMEM((units, CB, width), jnp.bfloat16),
+            pltpu.VMEM((units, windows - 1, rows_here, width), jnp.bfloat16),
+            pltpu.VMEM((units, rows_here, width), jnp.float32),
+            pltpu.VMEM((2, blocks, units, rows_here, width), jnp.float32),
+            dma((3 + 2 * PIECES,)), dma((3 + 2 * PIECES,)), dma,
+            dma((units, windows - 1)), dma((units, windows - 1)),
+            dma((units, blocks - 1)), dma((units, blocks - 1)),
+            dma((units, blocks)), dma((units, blocks)),
         ],
         compiler_params=pltpu.CompilerParams(
             collective_id=0, has_side_effects=True, vmem_limit_bytes=48 * 1024 * 1024

time: 71 us -> 71.5 us (level)
  the two profiles are of different devices: /device:TPU:15 before, /device:TPU:0 now
where the time goes in v5:
time: 71.5 us; the launch traced here: 71.1 us
  Pallas kernels  68.2 us (95%)
  local copies, waits for them, and re-layouts  2.02 us (3%)
  other arithmetic  0.94 us (1%)
    pallas_call x1, Pallas kernels, shards(): pl.pallas_call(functools.partial(correlate_kernel, blocks, windows), out_...  52 us
    pallas_call x1, Pallas kernels, transform(): pl.pallas_call(transform_kernel, grid=(F // BINS,), out_shape=jax.ShapeDt...  16.1 us
    unnamed x9, local copies, waits for them, and re-layouts  2.02 us

profile of v5, /device:TPU:0, one launch (start us, length us, event | category | flops | bytes accessed | tf_op | source)
XLA Modules:
  0.0 71.1 jit_solution(11438464854863219457)
XLA Ops:
  0.0 0.0 copy-start
  0.0 0.0 copy-start.1
  0.0 0.0 copy-start.2
  0.0 0.9 %convert_multiply_fusion.weights = f32[2,64,256]{2,1,0:T(8,128)S(1)} fusion(s32[2,256,256]{2,1,0:T(8,128)} %param.9, s32[]{:T(128)S(6)} %select_n.3), kind=kLoop, calls=%fused_computation | loop fusion | flops 65536 | bytes 262148 | tf_op jit(solution)/shard_map/mul | solution.py:347
  0.9 16.1 %shard_map.73.white = bf16[128,4096]{1,0:T(8,128)(2,1)} custom-call(bf16[1,128,8192]{2,1,0:T(8,128)(2,1)} %signal.1, f32[1,8192]{1,0:T(1,128)} %constant.20.clone.window, bf16[8,2048,512]{2,1,0:T(8,128)(2,1)} %constant.21.clone.table), custom_call_target="tpu_custom_call" | custom-call | flops 8999999488 | bytes 20000000 | tf_op jit(solution)/shard_map/pallas_call | solution.py:92
  17.1 0.0 copy-done
  17.1 0.0 copy-done.1
  17.1 0.0 copy-done.2
  17.1 0.0 copy-start.3
  17.1 1.2 %copy-done.3 = bf16[128,4096]{1,0:T(8,128)(2,1)S(1)} copy-done((bf16[128,4096]{1,0:T(8,128)(2,1)S(1)}, bf16[128,4096]{1,0:T(8,128)(2,1)}, u32[]{:S(2)}) %copy-start.3) | copy-done | bytes 1048600
  18.3 52.0 %shard_map.74 = f32[2,64,1024]{2,1,0:T(8,128)S(1)} custom-call(bf16[128,4096]{1,0:T(8,128)(2,1)S(1)} %copy-done.3, s32[2,2]{1,0:T(2,128)S(1)} %copy-done, f32[2,64,256]{2,1,0:T(8,128)S(1)} %convert_multiply_fusion.weights, f32[4,2048]{1,0:T(4,128)S(1)} %copy-done.2, f32[4,2048]{1,0:T(4,128)S(1)} %copy-done.1), custom_call_target="tpu_custom_call" | custom-call | flops 5000000000 | bytes 4000000 | tf_op jit(solution)/shard_map/pallas_call | solution.py:353
  70.3 0.8 %copy.9 = f32[2,64,1024]{2,1,0:T(8,128)} copy(f32[2,64,1024]{2,1,0:T(8,128)S(1)} %shard_map.74) | data formatting | bytes 1048576
Async XLA Ops:
  0.0 17.1 %copy-start = (s32[2,2]{1,0:T(2,128)S(1)}, s32[2,2]{1,0:T(2,128)}, u32[]{:S(2)}) copy-start(s32[2,2]{1,0:T(2,128)} %pairs.1) | copy-start | bytes 52
  0.0 17.1 %copy-start.1 = (f32[4,2048]{1,0:T(4,128)S(1)}, f32[4,2048]{1,0:T(4,128)}, u32[]{:S(2)}) copy-start(f32[4,2048]{1,0:T(4,128)} %constant.23.clone.sines) | copy-start | bytes 98308
  0.0 17.1 %copy-start.2 = (f32[4,2048]{1,0:T(4,128)S(1)}, f32[4,2048]{1,0:T(4,128)}, u32[]{:S(2)}) copy-start(f32[4,2048]{1,0:T(4,128)} %constant.22.clone.cosines) | copy-start | bytes 98308
  17.1 1.2 %copy-start.3 = (bf16[128,4096]{1,0:T(8,128)(2,1)S(1)}, bf16[128,4096]{1,0:T(8,128)(2,1)}, u32[]{:S(2)}) copy-start(bf16[128,4096]{1,0:T(8,128)(2,1)} %shard_map.73.white) | copy-start | bytes 3145732
